TPU v7x, 128 devices: a whole 4x4x4 slice. The times are simulated.
128 devices in a mesh: rows: 8 (over x, z_lo), cols: 16 (over z_hi, y, core).
Axes of the slice: x: 4, y: 4, z: 4 (z_hi: 2, z_lo: 2; z = z_hi * 2 + z_lo), core: 2. Of those that a mesh axis runs over, the one named last changes fastest.
Arguments:
- spectra: bfloat16 [4096, 4096], P(('rows', 'cols')), may hold values from -6 to 6
- band_weights: float32 [2048], replicated, may hold values from 0.3 to 3
- lag_weights: float32 [4], replicated, may hold values from 0.5 to 2
- selected_bins: int32 [8], replicated, may hold values from 0 to 31
Outputs:
- correlations: float32 [4, 4096, 4096], P(None, 'rows', 'cols')
- gradient: float32 [4096, 4096], P(('rows', 'cols'))
All inputs are finite; a program needn't handle non-finite values.
Results may differ from a plain program's by a relative error of at most 0.0045.
Values may be sent and summed in bfloat16 or wider, within the bound.
A program may use at most 128 MiB of HBM per device.

v0:
```python
import jax
import jax.numpy as jnp
from jax import lax
from jax.sharding import PartitionSpec as P

LAGS = 4
LAG_STEP = 8
BIN = 128


def spread(block, axis, owner):
    block = jnp.where(lax.axis_index(axis) == owner, block, jnp.zeros_like(block))
    return lax.psum(block, axis)


def per_device(spectra, band_weights, lag_weights, selected_bins):
    n_rows = lax.axis_size("rows")
    n_cols = lax.axis_size("cols")
    row_index = lax.axis_index("rows")
    col_index = lax.axis_index("cols")
    freqs = band_weights.shape[0]
    raw = spectra.astype(jnp.float32)
    mean_power = jnp.mean(raw * raw, axis=1, keepdims=True)
    bin_gains = jnp.concatenate([band_weights, band_weights])
    whitened = (raw * lax.rsqrt(mean_power + 1e-05) * bin_gains[None, :]).astype(jnp.bfloat16)
    row_tile = lax.all_gather(whitened, "cols", axis=0, tiled=True)
    row_len = row_tile.shape[0]
    fold_ratio = n_cols // n_rows
    col_len = row_len // fold_ratio
    slot_part = col_index % fold_ratio
    owner_row = col_index // fold_ratio
    own_piece = lax.dynamic_slice_in_dim(row_tile, slot_part * col_len, col_len, 0)
    col_tile = spread(own_piece, "rows", owner_row)
    row_chan = row_index * row_len + jnp.arange(row_len, dtype=jnp.int32)
    col_chan = col_index * col_len + jnp.arange(col_len, dtype=jnp.int32)
    distance = jnp.abs(row_chan[:, None] - col_chan[None, :]) // BIN
    selected = jnp.any(distance[:, :, None] == selected_bins[None, None, :], axis=2).astype(
        jnp.float32
    )
    norm_scale = 1.0 / jnp.sqrt(jnp.float32(2 * freqs))
    bin_index = jnp.arange(freqs, dtype=jnp.float32)
    real_part = row_tile[:, :freqs].astype(jnp.float32)
    imag_part = row_tile[:, freqs:].astype(jnp.float32)
    outputs = []
    row_grad = jnp.zeros((row_len, 2 * freqs), jnp.float32)
    col_grad = jnp.zeros((col_len, 2 * freqs), jnp.float32)
    for lag_index in range(LAGS):
        shift_lag = float((lag_index - LAGS // 2) * LAG_STEP)
        theta = jnp.pi * bin_index * shift_lag / freqs
        cosine = jnp.cos(theta)
        sine_part = jnp.sin(theta)
        rotated = jnp.concatenate(
            [
                real_part * cosine - imag_part * sine_part,
                imag_part * cosine + real_part * sine_part,
            ],
            axis=1,
        ).astype(jnp.bfloat16)
        correlation = (
            lax.dot_general(
                rotated, col_tile, (((1,), (1,)), ((), ())), preferred_element_type=jnp.float32
            )
            * norm_scale
        )
        outputs.append(correlation)
        adjoint = (lag_weights[lag_index] * selected * correlation).astype(jnp.bfloat16)
        back = jnp.dot(adjoint, col_tile, preferred_element_type=jnp.float32) * norm_scale
        back_real = back[:, :freqs]
        back_imag = back[:, freqs:]
        row_grad = row_grad + jnp.concatenate(
            [
                back_real * cosine + back_imag * sine_part,
                back_imag * cosine - back_real * sine_part,
            ],
            axis=1,
        )
        col_grad = (
            col_grad
            + lax.dot_general(
                adjoint, rotated, (((0,), (0,)), ((), ())), preferred_element_type=jnp.float32
            )
            * norm_scale
        )
    col_total = lax.psum(col_grad, "rows")
    is_owner = (owner_row == row_index).astype(jnp.float32)
    addition = lax.dynamic_update_slice_in_dim(
        jnp.zeros_like(row_grad), col_total * is_owner, slot_part * col_len, 0
    )
    gradient = lax.psum_scatter(row_grad + addition, "cols", scatter_dimension=0, tiled=True)
    return (jnp.stack(outputs), gradient)


def solution(mesh):
    placed = (P(("rows", "cols"), None), P(), P(), P())
    return jax.shard_map(
        per_device,
        mesh=mesh,
        in_specs=placed,
        out_specs=(P(None, "rows", "cols"), P(("rows", "cols"), None)),
        check_vma=False,
    )
```

profile of v0, /device:TPU:0, one launch (start us, length us, event | category | flops | bytes accessed | tf_op | source)
XLA Modules:
  0.0 497.7 jit_solution(1436570777540770167)
XLA Ops:
  7.2 0.0 copy-start.16
  7.2 0.0 all-gather.2.cloned.1.call-start
  7.2 1.1 fusion.28
  8.3 0.8 pad_maximum_fusion.21
  9.1 1.8 fusion.30
  10.9 0.0 all-gather.2.cloned.1.call-update
  10.9 0.0 all-reduce.3.cloned.1.call-start
  11.0 1.5 fusion.58
  12.5 0.1 fusion.40
  12.6 0.1 fusion.38
  12.6 0.1 fusion.36
  12.7 57.0 %all-gather.2.cloned.1.call-done = bf16[512,4096]{1,0:T(8,128)(2,1)} async-done(((bf16[32,4096]{1,0:T(8,128)(2,1)}), bf16[512,4096]{1,0:T(8,128)(2,1)}) %all-gather.2.cloned.1.call-update) | async-done | bytes 4194320 | tf_op jit(solution)/shard_map/all_gather | solution.py:26
  69.7 3.3 dynamic-slice_select_fusion
  73.0 0.0 all-reduce.3.cloned.1.call-update
  73.0 0.0 all-reduce.5.cloned.1.call-start
  73.1 0.1 fusion.34
  73.1 0.4 add_select_fusion
  73.6 0.0 copy-done.16
  73.6 1.7 compare_reduce_fusion
  75.3 0.0 copy-start.1
  75.3 6.1 %fusion.8 = (bf16[512,2048]{1,0:T(8,128)(2,1)}, bf16[512,2048]{1,0:T(8,128)(2,1)}) fusion(f32[2048]{0:T(1024)S(1)} %get-tuple-element.32, f32[2048]{0:T(1024)S(1)} %get-tuple-element.33, bf16[512,4096]{1,0:T(8,128)(2,1)} %all-gather.2.cloned.1.call-done), kind=kLoop, calls=%fused_computation.32 | loop fusion | flops 10485760 | bytes 8404992 | tf_op jit(solution)/shard_map/convert.4
  81.5 0.0 copy-done.1
  81.5 6.0 %fusion.4 = (bf16[512,2048]{1,0:T(8,128)(2,1)S(1)}, bf16[512,2048]{1,0:T(8,128)(2,1)}, bf16[512,2048]{1,0:T(8,128)(2,1)}, bf16[512,2048]{1,0:T(8,128)(2,1)}, bf1...) fusion(f32[2048]{0:T(1024)S(1)} %get-tuple-element.30, f32[2048]{0:T(1024)S(1)} %get-tuple-element.31, ...), kind=kLoop, calls=%fused_computation.28 | loop fusion | flops 27262976 | bytes 16826368 | tf_op jit(solution)/shard_map/convert.6
  87.5 89.1 %all-reduce.3.cloned.1.call-done = bf16[256,4096]{1,0:T(8,128)(2,1)} async-done(((bf16[256,4096]{1,0:T(8,128)(2,1)}), bf16[256,4096]{1,0:T(8,128)(2,1)}) %all-reduce.3.cloned.1.call-update) | async-done | bytes 2097168 | tf_op jit(solution)/shard_map/psum | solution.py:13
  176.5 3.7 fusion.24
  180.2 0.0 copy-done.11
  180.2 0.0 copy-start.13
  180.2 0.0 copy-done.12
  180.2 0.0 copy-start
  180.2 0.0 copy-start.6
  180.3 0.0 copy-start.7
  180.3 4.3 fusion.22
  184.6 0.0 copy-done.13
  184.6 0.0 copy-done
  184.6 1.3 fusion.25
  185.9 2.1 convolution_add_fusion.2
  188.0 0.1 copy-done.5
  188.1 1.3 fusion.26
  189.4 2.1 convolution_add_fusion.1
  191.6 0.1 copy-done.3
  191.7 1.3 fusion.27
  192.9 0.0 copy-start.8
  193.0 0.8 copy-done.8
  193.7 4.1 fusion.2
  197.9 0.0 all-reduce.5.cloned.1.call-update
  197.9 0.3 reduce-scatter.2.cloned.1.call-start
  198.2 0.0 copy-start.9
  198.2 5.2 %convolution_multiply_fusion.2 = f32[512,4096]{1,0:T(8,128)} fusion(bf16[256,4096]{1,0:T(8,128)(2,1)S(1)} %copy-done, f32[512,256]{1,0:T(8,128)S(1)} %fusion.25, pred[512,256]{1,0:T(8,128)(4,1)S(1)} %compare_reduce_fusion, f32[]{:T(128)} %bitcast.5), kind=kOutput, calls=%fused_computation.21 | convolution fusion | flops 1076232192 | bytes 11141124 | tf_op jit(solution)/shard_map/dot_general | solution.py:67
  203.4 0.0 copy-done.9
  203.4 5.2 %convolution_multiply_fusion = f32[512,4096]{1,0:T(8,128)} fusion(bf16[256,4096]{1,0:T(8,128)(2,1)S(1)} %copy-done, f32[512,256]{1,0:T(8,128)S(1)} %copy-done.9, pred[512,256]{1,0:T(8,128)(4,1)S(1)} %compare_reduce_fusion, f32[]{:T(128)} %bitcast.7), kind=kOutput, calls=%fused_computation.19 | convolution fusion | flops 1076232192 | bytes 11141124 | tf_op jit(solution)/shard_map/dot_general | solution.py:67
  208.6 2.0 convolution_multiply_fusion.1
  210.6 1.9 convolution_multiply_fusion.3
  212.5 8.8 %multiply_add_fusion.2 = (f32[512,2048]{1,0:T(8,128)}, f32[512,2048]{1,0:T(8,128)}) fusion(f32[512,4096]{1,0:T(8,128)} %convolution_multiply_fusion.2, f32[2048]{0:T(1024)S(1)} %get-tuple-element.32, f32[2048]{0:T(1024)S(1)} %get-tuple-element.33), kind=kLoop, calls=%fused_computation.53 | loop fusion | flops 6291456 | bytes 16793600 | tf_op jit(solution)/shard_map/add | solution.py:72
  221.2 8.8 %multiply_add_fusion = (f32[512,2048]{1,0:T(8,128)}, f32[512,2048]{1,0:T(8,128)}) fusion(f32[512,4096]{1,0:T(8,128)} %convolution_multiply_fusion, f32[2048]{0:T(1024)S(1)} %get-tuple-element.26, f32[2048]{0:T(1024)S(1)} %get-tuple-element.27), kind=kLoop, calls=%fused_computation.49 | loop fusion | flops 6291456 | bytes 16793600 | tf_op jit(solution)/shard_map/add | solution.py:72
  230.0 4.4 multiply_add_fusion.1
  234.4 4.5 multiply_add_fusion.3
  239.0 16.2 %fusion.1 = f32[512,4096]{1,0:T(8,128)} fusion(f32[512,2048]{1,0:T(8,128)} %get-tuple-element.9, f32[512,2048]{1,0:T(8,128)} %get-tuple-element.8, f32[512,2048]{1,0:T(8,128)} %get-tuple-element.7, f32[512,2048]{1,0:T(8,128)} %get-tuple-element.6, f32[512,2048]{1,0:T(8,128)} %get-tuple-element.5, f32[512,2048]{1,0:T(8,128)} %get-tuple-element.4, ...), kind=kLoop, calls=%fused_computation.18 | loop fusion | flops 14680064 | bytes 41943040 | tf_op jit(solution)/shard_map/add | solution.py:70
  255.2 124.5 %all-reduce.5.cloned.1.call-done = f32[256,4096]{1,0:T(8,128)} async-done(((f32[256,4096]{1,0:T(8,128)}), f32[256,4096]{1,0:T(8,128)}) %all-reduce.5.cloned.1.call-update) | async-done | bytes 4194320 | tf_op jit(solution)/shard_map/psum | solution.py:84
  379.7 6.2 %add_dynamic-update-slice_fusion = f32[512,4096]{1,0:T(8,128)} fusion(f32[512,4096]{1,0:T(8,128)} %fusion.1, s32[]{:T(128)S(6)} %select_n.35, f32[256,4096]{1,0:T(8,128)} %all-reduce.5.cloned.1.call-done, f32[]{:T(128)S(6)} %convert_element_type.40), kind=kLoop, calls=%fused_computation.47 | loop fusion | flops 2097152 | bytes 12582920 | tf_op jit(solution)/shard_map/add | solution.py:89
  385.9 0.0 reduce-scatter.2.cloned.1.call-update
  385.9 1.0 copy-done.10
  387.0 0.2 copy-done.15
  387.1 1.5 pad_maximum_fusion.12
  388.6 102.5 %reduce-scatter.2.cloned.1.call-done = f32[32,4096]{1,0:T(8,128)} async-done(((f32[512,4096]{1,0:T(8,128)}), f32[32,4096]{1,0:T(8,128)}) %reduce-scatter.2.cloned.1.call-update) | async-done | bytes 524304 | tf_op jit(solution)/shard_map/reduce_scatter | solution.py:89
  (17 shorter events, 0.0 us)
Async XLA Ops:
  7.2 66.4 %copy-start.16 = (s32[8]{0:T(128)S(1)}, s32[8]{0:T(128)}, u32[]{:S(2)}) copy-start(s32[8]{0:T(128)} %param.7) | copy-start | bytes 100
  7.2 62.5 %all-gather.2.cloned.1.call-start = ((), (), s32[]{:S(2)}) async-start(), calls=%async_computation.1 | async-start | bytes 4456448 | tf_op jit(solution)/shard_map/all_gather | solution.py:26
  10.9 165.6 %all-reduce.3.cloned.1.call-start = ((), (), s32[]{:S(2)}) async-start(), calls=%async_computation.2 | async-start | bytes 4194304 | tf_op jit(solution)/shard_map/psum | solution.py:13
  73.0 306.7 %all-reduce.5.cloned.1.call-start = ((), (), s32[]{:S(2)}) async-start(), calls=%async_computation.3 | async-start | bytes 8388608 | tf_op jit(solution)/shard_map/psum | solution.py:84
  75.3 6.1 %copy-start.1 = (bf16[512,4096]{1,0:T(8,128)(2,1)S(1)}, bf16[512,4096]{1,0:T(8,128)(2,1)}, u32[]{:S(2)}) copy-start(bf16[512,4096]{1,0:T(8,128)(2,1)} %all-gather.2.cloned.1.call-done) | copy-start | bytes 12582916
  87.5 92.7 %copy-start.11 = (bf16[512,2048]{1,0:T(8,128)(2,1)}, bf16[512,2048]{1,0:T(8,128)(2,1)S(1)}, u32[]{:S(2)}) copy-start(bf16[512,2048]{1,0:T(8,128)(2,1)S(1)} %get-tuple-element.10) | copy-start | bytes 6291460
  176.5 3.7 copy-start.12
  180.2 4.4 copy-start.13
  180.2 4.4 copy-start
  180.2 4.4 copy-start.6
  180.3 4.4 copy-start.7
  185.9 2.1 copy-start.4
  185.9 2.2 copy-start.5
  189.4 2.1 copy-start.2
  189.4 2.2 copy-start.3
  192.9 0.8 copy-start.8
  197.9 293.2 %reduce-scatter.2.cloned.1.call-start = ((), (), s32[]{:S(2)}) async-start(), calls=%async_computation.4 | async-start | bytes 8912896 | tf_op jit(solution)/shard_map/reduce_scatter | solution.py:89
  198.2 5.2 %copy-start.9 = (f32[512,256]{1,0:T(8,128)S(1)}, f32[512,256]{1,0:T(8,128)}, u32[]{:S(2)}) copy-start(f32[512,256]{1,0:T(8,128)} %copy-done.8) | copy-start | bytes 1572868
  208.6 2.0 copy-start.14
  385.9 1.0 copy-start.10
  385.9 1.2 copy-start.15
Sparse Core Ops, SparseCore 0:
  11.0 58.5 all-gather.1
  73.1 103.3 all-reduce.2
  198.0 181.6 all-reduce.4
  386.1 105.0 reduce-scatter.1
where the time goes:
time: 498 us
  waiting for transfers between devices  373 us (75%)
  other arithmetic  72 us (14%)
  matrix products  34.4 us (7%)
  between operations  14.1 us (3%)
    psum x1, waiting for transfers between devices, per_device(): col_total = lax.psum(col_grad, 'rows')  124 us
    reduce_scatter x1, waiting for transfers between devices, per_device(): lax.psum_scatter(row_grad + addition, 'cols', scatter_dimension=0, tiled=...  103 us
    psum x1, waiting for transfers between devices, spread(): return lax.psum(block, axis)  89.1 us
    all_gather x1, waiting for transfers between devices, per_device(): row_tile = lax.all_gather(whitened, 'cols', axis=0, tiled=True)  57 us
    add x4, other arithmetic, per_device(): back_real * cosine + back_imag * sine_part  26.5 us
    add x1, other arithmetic, per_device(): row_grad + jnp.concatenate([back_real * cosine + back_imag * sine_part, b...  16.2 us
    dot_general x4, matrix products, per_device(): jnp.dot(adjoint, col_tile, preferred_element_type=jnp.float32) * norm_scale  14.2 us
    dot_general x4, matrix products, per_device(): lax.dot_general(adjoint, rotated, (((0,), (0,)), ((), ())), preferred_ele...  12.6 us
  transfers between devices with their start and end apart: 4, of which 4 were waited for; matrix products, arithmetic and copies ran while one was open for 15% of the time, Pallas kernels for 0%

commit v1 on v0

v1 whole, which is shorter than its diff:
```python
import functools

import jax
import jax.numpy as jnp
import numpy as np
from jax import lax
from jax.experimental import pallas as pl
from jax.experimental.pallas import tpu as pltpu
from jax.sharding import PartitionSpec as P

MESH = pl.DeviceIdType.MESH
LAG_STEP = 8
BIN = 128
NSEL = 8
NA = 5
C = 4096
F = 2048
NP = 4
B = F // NP
B2 = 2 * B
CH = 32
TR = 2 * 4 * 2 * CH
TC = 4 * 2 * CH
EPS = 1e-05
SCALE = 1.0 / np.sqrt(2.0 * F)

ZX, YP, YM, YFP, YFM, SB = 0, 1, 2, 3, 4, 5
PM, ZL, XP, XM, XFP, XFM = 6, 7, 8, 9, 10, 11
GS, G1P, G1M, G2P, G2M, G3 = 12, 13, 14, 15, 16, 17
NK = 18


def tables():
    theta = np.pi * np.arange(F) * LAG_STEP / F
    rows = np.stack([np.cos(theta), np.sin(theta), np.cos(2 * theta), np.sin(2 * theta)])
    return rows.reshape(4, NP, 1, B).transpose(1, 0, 2, 3).astype(np.float32)


def kernel(
    lagw_ref, bins_ref, spec_ref, gain_ref, tab_ref, corr_ref, grad_ref,
    row, col, acc, sel, adj, part, s_gs, r_gs, s_g1, r_g1, s_g2, r_g2, s_g3, r_g3, fin,
    ssem, rsem, osem,
):
    r = lax.axis_index("rows")
    c = lax.axis_index("cols")
    x, zl, zh, y, k = r // 2, r % 2, c // 8, (c // 2) % 4, c % 2
    y1, y2, y3 = (y + 1) % 4, (y + 2) % 4, (y + 3) % 4
    x1, x3 = (x + 1) % 4, (x + 3) % 4

    def at(x_, zl_, zh_, y_, k_):
        return (x_ * 2 + zl_, zh_ * 8 + y_ * 2 + k_)

    xs, zs = c // 4, (c // 2) % 2
    yy = (x - xs + 4) % 4
    kk = (zl + zs + k + 1) % 2
    yy1, yy2, yy3 = (yy + 1) % 4, (yy + 2) % 4, (yy + 3) % 4
    to_perm = at((y + x) % 4, (zl + k + zh + 1) % 2, r // 4, r % 4, zh)
    from_perm = at(xs, zs, k, yy, kk)
    d_zx = at(x, zl, 1 - zh, y, k)
    d_yp = at(x, zl, zh, y1, k)
    d_ym = at(x, zl, zh, y3, k)
    d_sb = at(x, zl, zh, y, 1 - k)
    d_zl = at(x, 1 - zl, zh, y, k)
    d_xp = at(x1, zl, zh, y, k)
    d_xm = at(x3, zl, zh, y, k)

    barrier = pltpu.get_barrier_semaphore()
    both = (d_zx, d_yp, d_ym, d_sb, d_zl, d_xp, d_xm)
    for d in both + (from_perm,):
        pl.semaphore_signal(barrier, inc=1, device_id=d, device_id_type=MESH)

    raw = spec_ref[...].astype(jnp.float32)
    power = jnp.mean(raw * raw, axis=1, keepdims=True)
    inv = lax.rsqrt(power + EPS)
    for p in range(NP):
        for h in range(2):
            s = slice(h * F + p * B, h * F + (p + 1) * B)
            g = gain_ref[:, p * B : (p + 1) * B]
            v = spec_ref[:, s].astype(jnp.float32) * inv * g
            row[p, zh, y, k, :, h * B : (h + 1) * B] = v.astype(jnp.bfloat16)

    pl.semaphore_wait(barrier, len(both) + 1)

    def send(kind, p, src, dst, dev):
        pltpu.make_async_remote_copy(
            src_ref=src, dst_ref=dst, send_sem=ssem.at[kind, p], recv_sem=rsem.at[kind, p],
            device_id=dev, device_id_type=MESH,
        ).start()

    def got(kind, p, dst):
        pltpu.make_async_copy(dst, dst, rsem.at[kind, p]).wait()

    def sent(kind, p, src):
        pltpu.make_async_copy(src, src, ssem.at[kind, p]).wait()

    for p in range(NP):
        own = row.at[p, zh, y, k]
        send(ZX, p, own, own, d_zx)
        send(PM, p, own, col.at[p, 2, y, k], to_perm)

    bits = jnp.int32(0)
    for e in range(NSEL):
        bits = bits | (jnp.int32(1) << bins_ref[e])

    def mask_rows(i, carry):
        ri = r * TR + i * 64 + lax.broadcasted_iota(jnp.int32, (64, TC), 0)
        ci = c * TC + lax.broadcasted_iota(jnp.int32, (64, TC), 1)
        dist = lax.shift_right_logical(jnp.abs(ri - ci), 7)
        hit = lax.shift_right_logical(jnp.full((64, TC), bits, jnp.int32), dist) & 1
        sel[pl.ds(pl.multiple_of(i * 64, 64), 64), :] = hit.astype(jnp.float32)
        return carry

    lax.fori_loop(0, TR // 64, mask_rows, 0)

    def stage1(p):
        got(PM, p, col.at[p, 2, yy, kk])
        mine = col.at[p, 2, yy, kk]
        send(ZL, p, mine, mine, d_zl)
        got(ZX, p, row.at[p, 1 - zh, y, k])
        mine = row.at[p, :, y, k]
        send(YP, p, mine, mine, d_yp)
        send(YM, p, mine, mine, d_ym)
        got(ZL, p, col.at[p, 2, yy, 1 - kk])
        mine = col.at[p, 2, yy]
        send(XP, p, mine, mine, d_xp)
        send(XM, p, mine, mine, d_xm)

    def stage2(p):
        got(YP, p, row.at[p, :, y3, k])
        blk = row.at[p, 0, y3, k]
        send(YFP, p, blk, blk, d_yp)
        got(YM, p, row.at[p, :, y1, k])
        blk = row.at[p, 1, y1, k]
        send(YFM, p, blk, blk, d_ym)
        got(XP, p, col.at[p, 2, yy3])
        blk = col.at[p, 2, yy3, 0]
        send(XFP, p, blk, blk, d_xp)
        got(XM, p, col.at[p, 2, yy1])
        blk = col.at[p, 2, yy1, 1]
        send(XFM, p, blk, blk, d_xm)

    def stage3(p):
        got(YFP, p, row.at[p, 0, y2, k])
        got(YFM, p, row.at[p, 1, y2, k])
        blk = row.at[p, :, :, k]
        send(SB, p, blk, blk, d_sb)
        got(XFP, p, col.at[p, 2, yy2, 0])
        got(XFM, p, col.at[p, 2, yy2, 1])

        def rot(i, carry):
            a, b = i // 2, i % 2
            v = col[p, 2, a, b]
            re = v[:, :B].astype(jnp.float32)
            im = v[:, B:].astype(jnp.float32)
            for t, (near, far) in enumerate(((1, 3), (0, 4))):
                cs = tab_ref[p, 2 * t]
                sn = tab_ref[p, 2 * t + 1]
                rc, rs, ic, is_ = re * cs, re * sn, im * cs, im * sn
                col[p, far, a, b, :, :B] = (rc + is_).astype(jnp.bfloat16)
                col[p, far, a, b, :, B:] = (ic - rs).astype(jnp.bfloat16)
                col[p, near, a, b, :, :B] = (rc - is_).astype(jnp.bfloat16)
                col[p, near, a, b, :, B:] = (ic + rs).astype(jnp.bfloat16)
            return carry

        lax.fori_loop(0, 8, rot, 0)

    def stage4(p):
        got(SB, p, row.at[p, :, :, 1 - k])

        def corr(a, carry):
            left = row[p].reshape(TR, B2)
            right = col[p, a].reshape(TC, B2)
            d = lax.dot_general(
                left, right, (((1,), (1,)), ((), ())), preferred_element_type=jnp.float32
            )
            if p == 0:
                acc[a] = d
            else:
                acc[a] += d
            return carry

        lax.fori_loop(0, NA, corr, 0)

    for t in range(NP + 3):
        for lag, stage in enumerate((stage1, stage2, stage3, stage4)):
            if 0 <= t - lag < NP:
                stage(t - lag)

    w0, w8, w16 = 2.0 * lagw_ref[2], lagw_ref[1] + lagw_ref[3], lagw_ref[0]
    for a, w in enumerate((w16, w8, w0, w8, w16)):

        def adjoint(i, carry):
            rows = pl.ds(pl.multiple_of(i * 64, 64), 64)
            v = acc[a, rows, :] * jnp.float32(SCALE)
            if a < 4:
                acc[a, rows, :] = v
            adj[rows, a * TC : (a + 1) * TC] = (v * (sel[rows, :] * w)).astype(jnp.bfloat16)
            return carry

        lax.fori_loop(0, TR // 64, adjoint, 0)
    outs = [pltpu.make_async_copy(acc.at[a], corr_ref.at[a], osem.at[a]) for a in range(4)]
    for o in outs:
        o.start()

    def grad0(p):
        def tile(n, carry):
            cols = pl.ds(pl.multiple_of(n * 256, 256), 256)
            d = jnp.dot(
                adj[...], col[p, :, :, :, :, cols].reshape(NA * TC, 256),
                preferred_element_type=jnp.float32,
            )
            part[p, :, :, :, :, cols] = d.reshape(2, 4, 2, CH, 256)
            return carry

        lax.fori_loop(0, B2 // 256, tile, 0)
        s_gs[p] = part[p, :, :, 1 - k].astype(jnp.bfloat16)
        send(GS, p, s_gs.at[p], r_gs.at[p], d_sb)

    def mine_at(p, h, yt):
        return part[p, h, yt, k] + r_gs[p, h, yt].astype(jnp.float32)

    def grad1(p):
        got(GS, p, r_gs.at[p])
        s_g1[p, 0] = mine_at(p, 0, y2).astype(jnp.bfloat16)
        send(G1P, p, s_g1.at[p, 0], r_g1.at[p, 0], d_yp)
        s_g1[p, 1] = mine_at(p, 1, y2).astype(jnp.bfloat16)
        send(G1M, p, s_g1.at[p, 1], r_g1.at[p, 1], d_ym)

    def grad2(p):
        got(G1P, p, r_g1.at[p, 0])
        s_g2[p, 0, 0] = (mine_at(p, 0, y1) + r_g1[p, 0].astype(jnp.float32)).astype(jnp.bfloat16)
        s_g2[p, 0, 1] = mine_at(p, 1, y1).astype(jnp.bfloat16)
        send(G2P, p, s_g2.at[p, 0], r_g2.at[p, 0], d_yp)
        got(G1M, p, r_g1.at[p, 1])
        s_g2[p, 1, 0] = mine_at(p, 0, y3).astype(jnp.bfloat16)
        s_g2[p, 1, 1] = (mine_at(p, 1, y3) + r_g1[p, 1].astype(jnp.float32)).astype(jnp.bfloat16)
        send(G2M, p, s_g2.at[p, 1], r_g2.at[p, 1], d_ym)

    def total_at(p, h):
        return (
            mine_at(p, h, y)
            + r_g2[p, 0, h].astype(jnp.float32)
            + r_g2[p, 1, h].astype(jnp.float32)
        )

    def grad3(p):
        got(G2P, p, r_g2.at[p, 0])
        got(G2M, p, r_g2.at[p, 1])
        s_g3[p] = total_at(p, 1 - zh).astype(jnp.bfloat16)
        send(G3, p, s_g3.at[p], r_g3.at[p], d_zx)
        fin[p] = total_at(p, zh)

    def grad4(p):
        got(G3, p, r_g3.at[p])
        v = (fin[p] + r_g3[p].astype(jnp.float32)) * jnp.float32(SCALE)
        grad_ref[:, p * B : (p + 1) * B] = v[:, :B]
        grad_ref[:, F + p * B : F + (p + 1) * B] = v[:, B:]

    for t in range(NP + 4):
        for lag, stage in enumerate((grad0, grad1, grad2, grad3, grad4)):
            if 0 <= t - lag < NP:
                stage(t - lag)

    for p in range(NP):
        for kind, src in (
            (ZX, row.at[p, zh, y, k]), (PM, row.at[p, zh, y, k]),
            (YP, row.at[p, :, y, k]), (YM, row.at[p, :, y, k]),
            (YFP, row.at[p, 0, y3, k]), (YFM, row.at[p, 1, y1, k]),
            (SB, row.at[p, :, :, k]), (ZL, col.at[p, 2, yy, kk]),
            (XP, col.at[p, 2, yy]), (XM, col.at[p, 2, yy]),
            (XFP, col.at[p, 2, yy3, 0]), (XFM, col.at[p, 2, yy1, 1]),
            (GS, s_gs.at[p]), (G1P, s_g1.at[p, 0]), (G1M, s_g1.at[p, 1]),
            (G2P, s_g2.at[p, 0]), (G2M, s_g2.at[p, 1]), (G3, s_g3.at[p]),
        ):
            sent(kind, p, src)
    for o in outs:
        o.wait()


def per_device(spectra, band_weights, lag_weights, selected_bins):
    bf16, f32 = jnp.bfloat16, jnp.float32
    smem = pl.BlockSpec(memory_space=pltpu.SMEM)
    vmem = pl.BlockSpec(memory_space=pltpu.VMEM)
    return pl.pallas_call(
        kernel,
        out_shape=(
            jax.ShapeDtypeStruct((4, TR, TC), f32),
            jax.ShapeDtypeStruct((CH, 2 * F), f32),
        ),
        in_specs=[smem, smem, vmem, vmem, vmem],
        out_specs=(pl.BlockSpec(memory_space=pl.ANY), vmem),
        scratch_shapes=[
            pltpu.VMEM((NP, 2, 4, 2, CH, B2), bf16),
            pltpu.VMEM((NP, NA, 4, 2, CH, B2), bf16),
            pltpu.VMEM((NA, TR, TC), f32),
            pltpu.VMEM((TR, TC), f32),
            pltpu.VMEM((TR, NA * TC), bf16),
            pltpu.VMEM((NP, 2, 4, 2, CH, B2), f32),
            pltpu.VMEM((NP, 2, 4, CH, B2), bf16),
            pltpu.VMEM((NP, 2, 4, CH, B2), bf16),
            pltpu.VMEM((NP, 2, CH, B2), bf16),
            pltpu.VMEM((NP, 2, CH, B2), bf16),
            pltpu.VMEM((NP, 2, 2, CH, B2), bf16),
            pltpu.VMEM((NP, 2, 2, CH, B2), bf16),
            pltpu.VMEM((NP, CH, B2), bf16),
            pltpu.VMEM((NP, CH, B2), bf16),
            pltpu.VMEM((NP, CH, B2), f32),
            pltpu.SemaphoreType.DMA((NK, NP)),
            pltpu.SemaphoreType.DMA((NK, NP)),
            pltpu.SemaphoreType.DMA((4,)),
        ],
        compiler_params=pltpu.CompilerParams(
            collective_id=0, has_side_effects=True, vmem_limit_bytes=60 * 2**20
        ),
        cost_estimate=pl.CostEstimate(
            flops=4 * TR * TC * NA * 2 * F, bytes_accessed=4 * TR * TC * 4, transcendentals=0
        ),
        name="noise_corr",
    )(lag_weights, selected_bins, spectra, band_weights.reshape(1, F), jnp.asarray(tables()))


def solution(mesh):
    placed = (P(("rows", "cols"), None), P(), P(), P())
    return jax.shard_map(
        per_device,
        mesh=mesh,
        in_specs=placed,
        out_specs=(P(None, "rows", "cols"), P(("rows", "cols"), None)),
        check_vma=False,
    )
```

time: 498 us -> 86.3 us (0.17)
  waiting for transfers between devices: 373 us -> 0 us
  Pallas kernels: 0 us -> 81.6 us
  other arithmetic: 72 us -> 0 us
  matrix products: 34.4 us -> 0 us
  between operations: 14.1 us -> 0.65 us
    psum x2 -> x0, waiting for transfers between devices: 214 us -> none  [the longest x1 124 us: per_device(): col_total = lax.psum(col_grad, 'rows')]
    reduce_scatter x1 -> x0, waiting for transfers between devices: 103 us -> none  [per_device(): lax.psum_scatter(row_grad + addition, 'cols', scatter_dimension=0, tiled=...]
    pallas_call x0 -> x1, Pallas kernels: none -> 81.6 us  [per_device(): pl.pallas_call(kernel, out_shape=(jax.ShapeDtypeStruct((4, TR, TC), f32),...]
    all_gather x1 -> x0, waiting for transfers between devices: 57 us -> none  [per_device(): row_tile = lax.all_gather(whitened, 'cols', axis=0, tiled=True)]
    add x8 -> x0, other arithmetic: 49 us -> none  [the longest x4 26.5 us: per_device(): back_real * cosine + back_imag * sine_part]
    dot_general x12 -> x0, matrix products: 34.4 us -> none  [the longest x4 14.2 us: per_device(): jnp.dot(adjoint, col_tile, preferred_element_type=jnp.float32) * norm_scale]
    another operation x3 -> x0, other arithmetic: 13.6 us -> none
  transfers between devices with their start and end apart: 4 -> 0, of which waited for: 4 -> 0; matrix products, arithmetic and copies ran while one was open for 15% -> 0% of each run, Pallas kernels for 0% -> 0%
where the time goes in v1:
time: 86.3 us; the launch traced here: 86.1 us
  Pallas kernels  81.6 us (95%)
  local copies, waits for them, and re-layouts  3.9 us (5%)
    pallas_call x1, Pallas kernels, per_device(): pl.pallas_call(kernel, out_shape=(jax.ShapeDtypeStruct((4, TR, TC), f32),...  81.6 us
    unnamed x4, local copies, waits for them, and re-layouts  3.9 us

profile of v1, /device:TPU:0, one launch (start us, length us, event | category | flops | bytes accessed | tf_op | source)
XLA Modules:
  0.0 86.1 jit_solution(6118571924582012175)
XLA Ops:
  0.6 81.6 %noise_corr.1 = (f32[4,512,256]{2,1,0:T(8,128)}, f32[32,4096]{1,0:T(8,128)}) custom-call(f32[4]{0:T(128)} %lagw_ref.1, s32[8]{0:T(128)} %bins_ref.1, bf16[32,4096]{1,0:T(8,128)(2,1)} %spec_ref.1, f32[1,2048]{1,0:T(1,128)} %bitcast.1, f32[4,4,1,512]{3,2,1,0:T(1,128)} %constant.2.clone.tab_ref), custom_call_target="tpu_custom_call" | custom-call | flops 10737418240 | bytes 2097152 | tf_op jit(solution)/shard_map/noise_corr/pallas_call | solution.py:284
  82.2 0.0 copy-start
  82.2 3.1 %copy.9 = f32[4,512,256]{2,1,0:T(8,128)} copy(f32[4,512,256]{2,1,0:T(8,128)} %get-tuple-element.4) | data formatting | bytes 4194304
  85.3 0.0 copy-done
  85.3 0.8 copy.10
Async XLA Ops:
  82.2 3.1 %copy-start = (f32[32,4096]{1,0:T(8,128)S(1)}, f32[32,4096]{1,0:T(8,128)}, u32[]{:S(2)}) copy-start(f32[32,4096]{1,0:T(8,128)} %get-tuple-element.5) | copy-start | bytes 1572868

commit v2 on v0

v2 whole, which is shorter than its diff:
```python
import functools

import jax
import jax.numpy as jnp
import numpy as np
from jax import lax
from jax.experimental import pallas as pl
from jax.experimental.pallas import tpu as pltpu
from jax.sharding import PartitionSpec as P

MESH = pl.DeviceIdType.MESH
LAG_STEP = 8
BIN = 128
NSEL = 8
NA = 5
C = 4096
F = 2048
NP = 4
B = F // NP
B2 = 2 * B
CH = 32
TR = 2 * 4 * 2 * CH
TC = 4 * 2 * CH
EPS = 1e-05
SCALE = 1.0 / np.sqrt(2.0 * F)

NPC = NP // 2

TURN = (0, 1, 4, 2, 3)

GROUPS = {
    "ZX": "ZX", "YPO": "YO", "YMO": "YO", "YPQ": "YQ", "YMQ": "YQ", "YFO": "YF", "YFQ": "YF",
    "SB": "SB", "PM": "PM", "ZL": "ZL", "XPO": "XO", "XMO": "XO", "XPQ": "XQ", "XMQ": "XQ",
    "XFO": "XF", "XFQ": "XF", "GS": "GS", "G1P": "G1", "G1M": "G1", "G2P0": "G2", "G2P1": "G2",
    "G2M0": "G2", "G2M1": "G2", "G3": "G3", "H1P": "H1", "H1M": "H1", "H2PO": "H2",
    "H2PQ": "H2", "H2MO": "H2", "H2MQ": "H2", "H4O": "H4", "H4Q": "H4", "H5": "H5",
}
KINDS = list(GROUPS)
ARRIVALS = sorted(set(GROUPS.values()))
NK, NG = len(KINDS), len(ARRIVALS)


def tables():
    theta = np.pi * np.arange(F) * LAG_STEP / F
    rows = np.stack([np.cos(theta), np.sin(theta), np.cos(2 * theta), np.sin(2 * theta)])
    return rows.reshape(4, NP, 1, B).transpose(1, 0, 2, 3).astype(np.float32)


def kernel(
    lagw_in, bins_in, spec_in, gain_in, tab_in, corr_ref, grad_ref,
    row, col, turned, acc, sel, adj, adjt, part, partc,
    s_gs, r_gs, s_g1, r_g1, s_g2, r_g2, s_g3, r_g3, fin,
    s_h1, r_h1, s_h2, r_h2, s_h4, r_h4, s_h5, r_h5, lagw_ref, bins_ref, spec_ref, gain_ref, tab_ref,
    ssem, rsem, hsem, osem, isem,
):
    ins = [
        pltpu.make_async_copy(src, dst, isem.at[i])
        for i, (src, dst) in enumerate((
            (spec_in, spec_ref), (gain_in, gain_ref), (bins_in, bins_ref),
            (lagw_in, lagw_ref), (tab_in, tab_ref),
        ))
    ]
    for copy in ins:
        copy.start()
    r = lax.axis_index("rows")
    c = lax.axis_index("cols")
    x, zl, zh, y, k = r // 2, r % 2, c // 8, (c // 2) % 4, c % 2
    y1, y2, y3 = (y + 1) % 4, (y + 2) % 4, (y + 3) % 4
    x1, x3 = (x + 1) % 4, (x + 3) % 4

    def at(x_, zl_, zh_, y_, k_):
        return (x_ * 2 + zl_, zh_ * 8 + y_ * 2 + k_)

    xs, zs = c // 4, (c // 2) % 2
    kk = (zl + zs + k + 1) % 2
    yy = (x + 15 - k - 2 * kk - 3 * (xs // 2)) % 4
    yy1, yy2, yy3 = (yy + 1) % 4, (yy + 2) % 4, (yy + 3) % 4
    xt, zt = (y + zh + 2 * k + 3 * (x // 2) + 1) % 4, (zl + k + zh) % 2
    to_perm, from_perm = at(xt, 1 - zt, r // 4, r % 4, zh), at(xs, zs, k, yy, kk)
    to_mid = [at(x, zs, k, v, (k + 1 + y // 2 + v // 2) % 2) for v in (yy, yy2)]
    turn = (x + 7 - zh - y) % 4
    zm = turn % 2
    km = ((turn + 4 - 3 * zm) % 4) // 2
    ym = 2 * ((k + zh + 1 + y // 2) % 2) + zl
    xm = 2 * zm + ym // 2
    from_rep = [at(x, h, zm, ym, zh) for h in range(2)]
    home = at(xm, zl, zh, y, km)
    at_home = (xm == x) & (km == k)
    from_mid = at(xt, zl, zh, y, (zh + 1 + (r % 4) // 2 + y // 2) % 2)
    via_self = (xt == x) & ((zh + 1 + (r % 4) // 2 + y // 2) % 2 == k)
    d_zx = at(x, zl, 1 - zh, y, k)
    d_yp = at(x, zl, zh, y1, k)
    d_ym = at(x, zl, zh, y3, k)
    d_sb = at(x, zl, zh, y, 1 - k)
    d_zl = at(x, 1 - zl, zh, y, k)
    d_xp = at(x1, zl, zh, y, k)
    d_xm = at(x3, zl, zh, y, k)
    ysrc, ydst = (y + 3 + 2 * zh) % 4, (y + 1 + 2 * zh) % 4
    xsrc, xdst = (x + 3 + 2 * kk) % 4, (x + 1 + 2 * kk) % 4
    yysrc = (yy + 3 + 2 * kk) % 4
    d_ys, d_yd = at(x, zl, zh, ysrc, k), at(x, zl, zh, ydst, k)
    d_xs, d_xd = at(xsrc, zl, zh, y, k), at(xdst, zl, zh, y, k)

    barrier = pltpu.get_barrier_semaphore()
    peers = [d_zx, d_yp, d_ym, d_sb, d_zl, d_xp, d_xm, from_perm] + from_rep
    for d in peers:
        pl.semaphore_signal(barrier, inc=1, device_id=d, device_id_type=MESH)

    @pl.when(jnp.logical_not(via_self))
    def _():
        pl.semaphore_signal(barrier, inc=1, device_id=from_mid, device_id_type=MESH)

    for copy in ins:
        copy.wait()
    raw = spec_ref[...].astype(jnp.float32)
    power = jnp.mean(raw * raw, axis=1, keepdims=True)
    inv = lax.rsqrt(power + EPS)
    for p in range(NP):
        for h in range(2):
            s = slice(h * F + p * B, h * F + (p + 1) * B)
            g = gain_ref[:, p * B : (p + 1) * B]
            v = spec_ref[:, s].astype(jnp.float32) * inv * g
            row[p, zh, y, k, :, h * B : (h + 1) * B] = v.astype(jnp.bfloat16)

    pl.semaphore_wait(barrier, jnp.where(at_home, len(peers), len(peers) + 1))

    def send(kind, p, src, dst, dev):
        i = KINDS.index(kind)
        pltpu.make_async_remote_copy(
            src_ref=src, dst_ref=dst, send_sem=ssem.at[i],
            recv_sem=rsem.at[ARRIVALS.index(GROUPS[kind]), p],
            device_id=dev, device_id_type=MESH,
        ).start()

    def got(group, p, dst):
        pltpu.make_async_copy(dst, dst, rsem.at[ARRIVALS.index(group), p]).wait()

    def sent(kinds, src):
        for kind in kinds:
            pltpu.make_async_copy(src, src, ssem.at[KINDS.index(kind)]).wait()

    def run(count, table):
        for t in range(count + max(skew for _, skew in table)):
            for fn, skew in table:
                if 0 <= t - skew < count:
                    fn(t - skew)

    bits = jnp.int32(0)
    for e in range(NSEL):
        bits = bits | (jnp.int32(1) << bins_ref[e])

    def mask(p):
        def mask_rows(i, carry):
            ri = r * TR + i * 64 + lax.broadcasted_iota(jnp.int32, (64, TC), 0)
            ci = c * TC + lax.broadcasted_iota(jnp.int32, (64, TC), 1)
            dist = lax.shift_right_logical(jnp.abs(ri - ci), 7)
            hit = lax.shift_right_logical(jnp.full((64, TC), bits, jnp.int32), dist) & 1
            sel[pl.ds(pl.multiple_of(i * 64, 64), 64), :] = hit.astype(jnp.float32)
            return carry

        if p == NP - 1:
            lax.fori_loop(0, TR // 64, mask_rows, 0)

    def pair(kind, p, blk, *devs):
        for way, dev in zip("PM", devs):
            send(kind[0] + way + kind[1], p, blk, blk, dev)

    def s_start(p):
        own = row.at[p, zh, y, k]
        send("PM", p, own, col.at[p, 2, y, k], to_perm)
        send("ZX", p, own, own, d_zx)
        pair("YO", p, own, d_yp, d_ym)

    def s_perm(p):
        blk = col.at[p, 2, yy, kk]
        got("PM", p, blk)
        send("ZL", p, blk, blk, d_zl)
        pair("XO", p, blk, d_xp, d_xm)

    def s_zx(p):
        blk = row.at[p, 1 - zh, y, k]
        got("ZX", p, blk)
        pair("YQ", p, blk, d_yp, d_ym)

    def s_zl(p):
        blk = col.at[p, 2, yy2, 1 - kk]
        got("ZL", p, blk)
        pair("XQ", p, blk, d_xp, d_xm)

    def f_yo(p):
        got("YO", p, row.at[p, :, y1, k])
        blk = row.at[p, zh, ysrc, k]
        send("YFO", p, blk, blk, d_yd)

    def f_xo(p):
        got("XO", p, col.at[p, 2, yy1])
        blk = col.at[p, 2, yysrc, kk]
        send("XFO", p, blk, blk, d_xd)

    def f_yq(p):
        got("YQ", p, row.at[p, :, y1, k])
        blk = row.at[p, 1 - zh, ydst, k]
        send("YFQ", p, blk, blk, d_ys)

    def f_xq(p):
        got("XQ", p, col.at[p, 2, yy1])
        blk = col.at[p, 2, yysrc, 1 - kk]
        send("XFQ", p, blk, blk, d_xs)

    def s_sib(p):
        got("YF", p, row.at[p, :, y2, k])
        blk = row.at[p, :, :, k]
        send("SB", p, blk, blk, d_sb)

    def g_xf(p):
        got("XF", p, col.at[p, 2, yy2])

    def g_sib(p):
        got("SB", p, row.at[p, :, :, 1 - k])

    def rotate(p, v, put):
        re = v[:, :B].astype(jnp.float32)
        im = v[:, B:].astype(jnp.float32)
        for t in range(2):
            cs, sn = tab_ref[p, 2 * t], tab_ref[p, 2 * t + 1]
            rc, rs, ic, is_ = re * cs, re * sn, im * cs, im * sn
            put(t, 0, (rc - is_).astype(jnp.bfloat16), (ic + rs).astype(jnp.bfloat16))
            put(t, 1, (rc + is_).astype(jnp.bfloat16), (ic - rs).astype(jnp.bfloat16))

    def rot(p):
        def body(i, carry):
            a, b = i // 2, i % 2

            def put(t, back, re, im):
                o = ((1, 3), (0, 4))[t][back]
                col[p, o, a, b, :, :B] = re
                col[p, o, a, b, :, B:] = im

            rotate(p, col[p, 2, a, b], put)
            return carry

        lax.fori_loop(0, 8, body, 0)

    def rot_first(p):
        def body(i, carry):
            h, a, b = i // 8, (i // 2) % 4, i % 2

            def put(t, back, re, im):
                o = ((2, 1), (3, 0))[t][back]
                turned[p, o, h, a, b, :, :B] = re
                turned[p, o, h, a, b, :, B:] = im

            rotate(p, row[p, h, a, b], put)
            return carry

        if p < NPC:
            lax.fori_loop(0, 16, body, 0)

    def correlate(p):
        left = row[p].reshape(TR, B2)
        for a in range(NA):
            d = lax.dot_general(
                left, col[p, a].reshape(TC, B2), (((1,), (1,)), ((), ())),
                preferred_element_type=jnp.float32,
            )
            if p > 0:
                d = acc[a] + d
            if p < NP - 1:
                acc[a] = d
                continue
            d = d * jnp.float32(SCALE)
            if a < 4:
                acc[a] = d
                outs[a].start()
            d = (d * (sel[...] * weights[a])).astype(jnp.bfloat16)
            adj[:, a * TC : (a + 1) * TC] = d
            adjt[TURN[a] * TR : (TURN[a] + 1) * TR, :] = d

    outs = [pltpu.make_async_copy(acc.at[a], corr_ref.at[a], osem.at[a]) for a in range(4)]
    w0, w8, w16 = 2.0 * lagw_ref[2], lagw_ref[1] + lagw_ref[3], lagw_ref[0]
    weights = (w16, w8, w0, w8, w16)
    run(NP, [
        (s_start, 0), (mask, 0), (s_perm, 1), (s_zx, 1), (f_yo, 1), (s_zl, 2), (f_xo, 2), (f_yq, 2),
        (f_xq, 3), (s_sib, 3), (g_xf, 4), (rot, 4), (g_sib, 4), (correlate, 4), (rot_first, 4),
    ])

    def f32(v):
        return v.astype(jnp.float32)

    def b16(v):
        return v.astype(jnp.bfloat16)

    def grad0(q):
        p = NPC + q

        d = jnp.dot(
            adj[...], col[p].reshape(NA * TC, B2), preferred_element_type=jnp.float32
        )
        part[q] = d.reshape(2, 4, 2, CH, B2)
        s_gs[q] = b16(part[q, :, :, 1 - k])
        send("GS", q, s_gs.at[q], r_gs.at[q], d_sb)

    def mine_at(q, h, yt):
        return part[q, h, yt, k] + f32(r_gs[q, h, yt])

    def reach(kind, q, src, dst, value, dev):
        src[...] = b16(value)
        send(kind, q, src, dst, dev)

    def grad1(q):
        got("GS", q, r_gs.at[q])
        reach("G1P", q, s_g1.at[q, 0], r_g1.at[q, 0], mine_at(q, 0, y2), d_yp)
        reach("G1M", q, s_g1.at[q, 1], r_g1.at[q, 1], mine_at(q, 1, y2), d_ym)
        reach("G2P1", q, s_g2.at[q, 0, 1], r_g2.at[q, 0, 1], mine_at(q, 1, y1), d_yp)
        reach("G2M0", q, s_g2.at[q, 1, 0], r_g2.at[q, 1, 0], mine_at(q, 0, y3), d_ym)

    def grad2(q):
        got("G1", q, r_g1.at[q])
        v = mine_at(q, 0, y1) + f32(r_g1[q, 0])
        reach("G2P0", q, s_g2.at[q, 0, 0], r_g2.at[q, 0, 0], v, d_yp)
        v = mine_at(q, 1, y3) + f32(r_g1[q, 1])
        reach("G2M1", q, s_g2.at[q, 1, 1], r_g2.at[q, 1, 1], v, d_ym)

    def grad3(q):
        def total_at(h):
            return mine_at(q, h, y) + f32(r_g2[q, 0, h]) + f32(r_g2[q, 1, h])

        got("G2", q, r_g2.at[q])
        s_g3[q] = b16(total_at(1 - zh))
        send("G3", q, s_g3.at[q], r_g3.at[q], d_zx)
        fin[q] = total_at(zh)

    def put_grad(p, v):
        v = v * jnp.float32(SCALE)
        grad_ref[:, p * B : (p + 1) * B] = v[:, :B]
        grad_ref[:, F + p * B : F + (p + 1) * B] = v[:, B:]

    def grad4(q):
        got("G3", q, r_g3.at[q])
        put_grad(NPC + q, fin[q] + f32(r_g3[q]))

    def colg0(q):
        def turned_dot(lags, right):
            return lax.dot_general(
                lags, right, (((0,), (0,)), ((), ())), preferred_element_type=jnp.float32
            )

        d = turned_dot(adjt[: 4 * TR, :], turned[q].reshape(4 * TR, B2))
        d += turned_dot(adjt[4 * TR :, :], row[q].reshape(TR, B2))
        partc[q] = d.reshape(4, 2, CH, B2)
        reach("H1P", q, s_h1.at[q, 0], r_h1.at[q, 0], partc[q, yy2, kk], d_xp)
        reach("H1M", q, s_h1.at[q, 1], r_h1.at[q, 1], partc[q, yy, 1 - kk], d_xm)
        reach("H2PQ", q, s_h2.at[q, 0, 1], r_h2.at[q, 0, 1], partc[q, yy3, 1 - kk], d_xp)
        reach("H2MO", q, s_h2.at[q, 1, 0], r_h2.at[q, 1, 0], partc[q, yy3, kk], d_xm)

    def colg1(q):
        got("H1", q, r_h1.at[q])
        v = partc[q, yy1, kk] + f32(r_h1[q, 0])
        reach("H2PO", q, s_h2.at[q, 0, 0], r_h2.at[q, 0, 0], v, d_xp)
        v = partc[q, yy1, 1 - kk] + f32(r_h1[q, 1])
        reach("H2MQ", q, s_h2.at[q, 1, 1], r_h2.at[q, 1, 1], v, d_xm)

    def colg2(q):
        got("H2", q, r_h2.at[q])
        v = partc[q, yy, kk] + f32(r_h2[q, 0, 0]) + f32(r_h2[q, 1, 0])
        reach("H4O", q, s_h4.at[q, 0], r_h4.at[q, 0], v, to_mid[0])
        v = partc[q, yy2, 1 - kk] + f32(r_h2[q, 0, 1]) + f32(r_h2[q, 1, 1])
        reach("H4Q", q, s_h4.at[q, 1], r_h4.at[q, 1], v, to_mid[1])

    def homeward(q):
        return pltpu.make_async_remote_copy(
            src_ref=s_h5.at[q], dst_ref=r_h5.at[q], send_sem=hsem.at[q],
            recv_sem=rsem.at[ARRIVALS.index("H5"), q], device_id=home, device_id_type=MESH,
        )

    def colg3(q):
        got("H4", q, r_h4.at[q])
        s_h5[q] = b16(f32(r_h4[q, 0]) + f32(r_h4[q, 1]))

        @pl.when(at_home)
        def _():
            r_h5[q] = s_h5[q]

        @pl.when(jnp.logical_not(at_home))
        def _():
            homeward(q).start()

    def colg4(q):
        @pl.when(jnp.logical_not(at_home))
        def _():
            homeward(q).wait_send()

        @pl.when(jnp.logical_not(via_self))
        def _():
            got("H5", q, r_h5.at[q])

        put_grad(q, f32(r_h5[q]))

    def settle():
        for kind in KINDS[: KINDS.index("GS")]:
            sent([kind], row.at[:, :, :, k] if kind == "SB" else row.at[:, zh, y, k])
        for o in outs:
            o.wait()

    for q in range(NPC):
        colg0(q)
        grad0(q)
    for n, fns in enumerate(((colg1, grad1), (colg2, grad2), (colg3, grad3), (colg4, grad4))):
        for q in range(NPC):
            for fn in fns:
                fn(q)
        if n == 0:
            settle()

    for kind in KINDS[KINDS.index("GS") : KINDS.index("H5")]:
        sent([kind], s_gs if kind == "GS" else s_h1.at[:, 0])


def per_device(spectra, band_weights, lag_weights, selected_bins):
    bf16, f32 = jnp.bfloat16, jnp.float32
    hbm = pl.BlockSpec(memory_space=pltpu.HBM)
    vmem = pl.BlockSpec(memory_space=pltpu.VMEM)
    return pl.pallas_call(
        kernel,
        out_shape=(
            jax.ShapeDtypeStruct((4, TR, TC), f32),
            jax.ShapeDtypeStruct((CH, 2 * F), f32),
        ),
        in_specs=[hbm] * 5,
        out_specs=(pl.BlockSpec(memory_space=pl.ANY), vmem),
        scratch_shapes=[
            pltpu.VMEM((NP, 2, 4, 2, CH, B2), bf16),
            pltpu.VMEM((NP, NA, 4, 2, CH, B2), bf16),
            pltpu.VMEM((NPC, 4, 2, 4, 2, CH, B2), bf16),
            pltpu.VMEM((NA, TR, TC), f32),
            pltpu.VMEM((TR, TC), f32),
            pltpu.VMEM((TR, NA * TC), bf16),
            pltpu.VMEM((NA * TR, TC), bf16),
            pltpu.VMEM((NPC, 2, 4, 2, CH, B2), f32),
            pltpu.VMEM((NPC, 4, 2, CH, B2), f32),
            pltpu.VMEM((NPC, 2, 4, CH, B2), bf16),
            pltpu.VMEM((NPC, 2, 4, CH, B2), bf16),
            pltpu.VMEM((NPC, 2, CH, B2), bf16),
            pltpu.VMEM((NPC, 2, CH, B2), bf16),
            pltpu.VMEM((NPC, 2, 2, CH, B2), bf16),
            pltpu.VMEM((NPC, 2, 2, CH, B2), bf16),
            pltpu.VMEM((NPC, CH, B2), bf16),
            pltpu.VMEM((NPC, CH, B2), bf16),
            pltpu.VMEM((NPC, CH, B2), f32),
            pltpu.VMEM((NPC, 2, CH, B2), bf16),
            pltpu.VMEM((NPC, 2, CH, B2), bf16),
            pltpu.VMEM((NPC, 2, 2, CH, B2), bf16),
            pltpu.VMEM((NPC, 2, 2, CH, B2), bf16),
            pltpu.VMEM((NPC, 2, CH, B2), bf16),
            pltpu.VMEM((NPC, 2, CH, B2), bf16),
            pltpu.VMEM((NPC, CH, B2), bf16),
            pltpu.VMEM((NPC, CH, B2), bf16),
            pltpu.SMEM((4,), f32),
            pltpu.SMEM((NSEL,), jnp.int32),
            pltpu.VMEM((CH, 2 * F), bf16),
            pltpu.VMEM((1, F), f32),
            pltpu.VMEM((NP, 4, 1, B), f32),
            pltpu.SemaphoreType.DMA((NK,)),
            pltpu.SemaphoreType.DMA((NG, NP)),
            pltpu.SemaphoreType.DMA((NPC,)),
            pltpu.SemaphoreType.DMA((4,)),
            pltpu.SemaphoreType.DMA((5,)),
        ],
        compiler_params=pltpu.CompilerParams(
            collective_id=0, has_side_effects=True, vmem_limit_bytes=58 * 2**20
        ),
        cost_estimate=pl.CostEstimate(
            flops=4 * TR * TC * NA * 2 * F, bytes_accessed=4 * TR * TC * 4, transcendentals=0
        ),
        name="noise_corr",
    )(lag_weights, selected_bins, spectra, band_weights.reshape(1, F), jnp.asarray(tables()))


def solution(mesh):
    placed = (P(("rows", "cols"), None), P(), P(), P())
    return jax.shard_map(
        per_device,
        mesh=mesh,
        in_specs=placed,
        out_specs=(P(None, "rows", "cols"), P(("rows", "cols"), None)),
        check_vma=False,
    )
```

time: 498 us -> 72.9 us (0.15)
  waiting for transfers between devices: 373 us -> 0 us
  other arithmetic: 72 us -> 0 us
  Pallas kernels: 0 us -> 67.5 us
  matrix products: 34.4 us -> 0 us
  between operations: 14.1 us -> 0.65 us
    psum x2 -> x0, waiting for transfers between devices: 214 us -> none  [the longest x1 124 us: per_device(): col_total = lax.psum(col_grad, 'rows')]
    reduce_scatter x1 -> x0, waiting for transfers between devices: 103 us -> none  [per_device(): lax.psum_scatter(row_grad + addition, 'cols', scatter_dimension=0, tiled=...]
    pallas_call x0 -> x1, Pallas kernels: none -> 67.5 us  [per_device(): pl.pallas_call(kernel, out_shape=(jax.ShapeDtypeStruct((4, TR, TC), f32),...]
    all_gather x1 -> x0, waiting for transfers between devices: 57 us -> none  [per_device(): row_tile = lax.all_gather(whitened, 'cols', axis=0, tiled=True)]
    add x8 -> x0, other arithmetic: 49 us -> none  [the longest x4 26.5 us: per_device(): back_real * cosine + back_imag * sine_part]
    dot_general x12 -> x0, matrix products: 34.4 us -> none  [the longest x4 14.2 us: per_device(): jnp.dot(adjoint, col_tile, preferred_element_type=jnp.float32) * norm_scale]
    another operation x3 -> x0, other arithmetic: 13.6 us -> none
  transfers between devices with their start and end apart: 4 -> 0, of which waited for: 4 -> 0; matrix products, arithmetic and copies ran while one was open for 15% -> 0% of each run, Pallas kernels for 0% -> 0%
where the time goes in v2:
time: 72.9 us; the launch traced here: 72 us
  Pallas kernels  67.5 us (93%)
  local copies, waits for them, and re-layouts  3.9 us (5%)
    pallas_call x1, Pallas kernels, per_device(): pl.pallas_call(kernel, out_shape=(jax.ShapeDtypeStruct((4, TR, TC), f32),...  67.5 us
    unnamed x4, local copies, waits for them, and re-layouts  3.9 us

profile of v2, /device:TPU:0, one launch (start us, length us, event | category | flops | bytes accessed | tf_op | source)
XLA Modules:
  0.0 72.0 jit_solution(1069379367233821625)
XLA Ops:
  0.6 67.5 %noise_corr.1 = (f32[4,512,256]{2,1,0:T(8,128)}, f32[32,4096]{1,0:T(8,128)}) custom-call(f32[4]{0:T(128)} %lagw_in.1, s32[8]{0:T(128)} %bins_in.1, bf16[32,4096]{1,0:T(8,128)(2,1)} %spec_in.1, f32[1,2048]{1,0:T(1,128)} %bitcast.1, f32[4,4,1,512]{3,2,1,0:T(1,128)} %constant.2.clone.tab_in), custom_call_target="tpu_custom_call" | custom-call | flops 10737418240 | bytes 2097152 | tf_op jit(solution)/shard_map/noise_corr/pallas_call | solution.py:423
  68.1 0.0 copy-start
  68.1 3.1 %copy.9 = f32[4,512,256]{2,1,0:T(8,128)} copy(f32[4,512,256]{2,1,0:T(8,128)} %get-tuple-element.4) | data formatting | bytes 4194304
  71.2 0.0 copy-done
  71.2 0.8 %copy.10 = f32[32,4096]{1,0:T(8,128)} copy(f32[32,4096]{1,0:T(8,128)S(1)} %copy-done) | data formatting | bytes 1048576
Async XLA Ops:
  68.1 3.1 %copy-start = (f32[32,4096]{1,0:T(8,128)S(1)}, f32[32,4096]{1,0:T(8,128)}, u32[]{:S(2)}) copy-start(f32[32,4096]{1,0:T(8,128)} %get-tuple-element.5) | copy-start | bytes 1572868

commit v3 on v2

--- a/solution.py
+++ b/solution.py
@@ -48,7 +48,7 @@
 
 def kernel(
     lagw_in, bins_in, spec_in, gain_in, tab_in, corr_ref, grad_ref,
-    row, col, turned, acc, sel, adj, adjt, part, partc,
+    row, col, turned, acc, short, sel, adj, adjt, part, partc,
     s_gs, r_gs, s_g1, r_g1, s_g2, r_g2, s_g3, r_g3, fin,
     s_h1, r_h1, s_h2, r_h2, s_h4, r_h4, s_h5, r_h5, lagw_ref, bins_ref, spec_ref, gain_ref, tab_ref,
     ssem, rsem, hsem, osem, isem,
@@ -270,13 +270,13 @@
                 continue
             d = d * jnp.float32(SCALE)
             if a < 4:
-                acc[a] = d
+                short[a] = d.astype(jnp.bfloat16)
                 outs[a].start()
             d = (d * (sel[...] * weights[a])).astype(jnp.bfloat16)
             adj[:, a * TC : (a + 1) * TC] = d
             adjt[TURN[a] * TR : (TURN[a] + 1) * TR, :] = d
 
-    outs = [pltpu.make_async_copy(acc.at[a], corr_ref.at[a], osem.at[a]) for a in range(4)]
+    outs = [pltpu.make_async_copy(short.at[a], corr_ref.at[a], osem.at[a]) for a in range(4)]
     w0, w8, w16 = 2.0 * lagw_ref[2], lagw_ref[1] + lagw_ref[3], lagw_ref[0]
     weights = (w16, w8, w0, w8, w16)
     run(NP, [
@@ -420,10 +420,10 @@
     bf16, f32 = jnp.bfloat16, jnp.float32
     hbm = pl.BlockSpec(memory_space=pltpu.HBM)
     vmem = pl.BlockSpec(memory_space=pltpu.VMEM)
-    return pl.pallas_call(
+    corr, grad = pl.pallas_call(
         kernel,
         out_shape=(
-            jax.ShapeDtypeStruct((4, TR, TC), f32),
+            jax.ShapeDtypeStruct((4, TR, TC), bf16),
             jax.ShapeDtypeStruct((CH, 2 * F), f32),
         ),
         in_specs=[hbm] * 5,
@@ -433,6 +433,7 @@
             pltpu.VMEM((NP, NA, 4, 2, CH, B2), bf16),
             pltpu.VMEM((NPC, 4, 2, 4, 2, CH, B2), bf16),
             pltpu.VMEM((NA, TR, TC), f32),
+            pltpu.VMEM((4, TR, TC), bf16),
             pltpu.VMEM((TR, TC), f32),
             pltpu.VMEM((TR, NA * TC), bf16),
             pltpu.VMEM((NA * TR, TC), bf16),
@@ -474,6 +475,7 @@
         ),
         name="noise_corr",
     )(lag_weights, selected_bins, spectra, band_weights.reshape(1, F), jnp.asarray(tables()))
+    return corr.astype(f32), grad
 
 
 def solution(mesh):

time: 72.9 us -> 74.9 us (1.027)
  local copies, waits for them, and re-layouts: 3.9 us -> 0.8 us
  other arithmetic: 0 us -> 2.78 us
  Pallas kernels: 67.5 us -> 69.7 us
    unnamed x4 -> x3, local copies, waits for them, and re-layouts: 3.9 us -> 0.8 us
    convert_element_type x0 -> x1, other arithmetic: none -> 2.78 us  [per_device(): return (corr.astype(f32), grad)]
    pallas_call x1, Pallas kernels: 67.5 us -> 69.7 us  [per_device(): pl.pallas_call(kernel, out_shape=(jax.ShapeDtypeStruct((4, TR, TC), bf16)...]
where the time goes in v3:
time: 74.9 us; the launch traced here: 73.9 us
  Pallas kernels  69.7 us (93%)
  other arithmetic  2.78 us (4%)
  local copies, waits for them, and re-layouts  0.8 us (1%)
    pallas_call x1, Pallas kernels, per_device(): pl.pallas_call(kernel, out_shape=(jax.ShapeDtypeStruct((4, TR, TC), bf16)...  69.7 us
    convert_element_type x1, other arithmetic, per_device(): return (corr.astype(f32), grad)  2.78 us

profile of v3, /device:TPU:0, one launch (start us, length us, event | category | flops | bytes accessed | tf_op | source)
XLA Modules:
  0.0 73.9 jit_solution(15991281896895879142)
XLA Ops:
  0.6 69.7 %noise_corr.1 = (bf16[4,512,256]{2,1,0:T(8,128)(2,1)}, f32[32,4096]{1,0:T(8,128)}) custom-call(f32[4]{0:T(128)} %lagw_in.1, s32[8]{0:T(128)} %bins_in.1, bf16[32,4096]{1,0:T(8,128)(2,1)} %spec_in.1, f32[1,2048]{1,0:T(1,128)} %bitcast.1, f32[4,4,1,512]{3,2,1,0:T(1,128)} %constant.2.clone.tab_in), custom_call_target="tpu_custom_call" | custom-call | flops 10737418240 | bytes 2097152 | tf_op jit(solution)/shard_map/noise_corr/pallas_call | solution.py:423
  70.3 0.0 copy-start
  70.3 2.8 %convert_element_type.3 = f32[4,512,256]{2,1,0:T(8,128)} convert(bf16[4,512,256]{2,1,0:T(8,128)(2,1)} %get-tuple-element.4) | non-fusion elementwise | flops 524288 | bytes 3145728 | tf_op jit(solution)/shard_map/convert_element_type | solution.py:478
  73.1 0.0 copy-done
  73.1 0.8 %copy.8 = f32[32,4096]{1,0:T(8,128)} copy(f32[32,4096]{1,0:T(8,128)S(1)} %copy-done) | data formatting | bytes 1048576
Async XLA Ops:
  70.3 2.8 %copy-start = (f32[32,4096]{1,0:T(8,128)S(1)}, f32[32,4096]{1,0:T(8,128)}, u32[]{:S(2)}) copy-start(f32[32,4096]{1,0:T(8,128)} %get-tuple-element.9) | copy-start | bytes 1572868
